TPU v7x, 32 devices: a whole 2x2x4 slice. The times are simulated.
32 devices in a mesh: lat: 8 (over z, core), freq: 4 (over y, x).
Axes of the slice: x: 2, y: 2, z: 4, core: 2. Of those that a mesh axis runs over, the one named last changes fastest.
Arguments:
- wavefield: float32 [2, 8, 2048, 2048], P(None, 'freq', 'lat'), may hold values from -6 to 6
- source_field: float32 [2, 8, 2048, 2048], P(None, 'freq', 'lat'), may hold values from -6 to 6
- slowness: float32 [2048, 2048], P('lat', 'freq'), may hold values from 0.00015 to 0.00094
- freq_index: int32 [8], P('freq'), may hold values from 192 to 767, as said below
Outputs:
- next_field: float32 [2, 8, 2048, 2048], P(None, 'freq', 'lat')
- image: float32 [2048, 2048], P('lat', 'freq')
Inputs may be any that keep to these rules, and one draw needn't show every extreme that they name: `freq_index`: distinct frequency indices.
All inputs are finite; a program needn't handle non-finite values.
Results may differ from a plain program's by a relative error of at most 0.00013.
Values sent between devices are 32-bit elements; how exact they have to be, the bound alone decides.
A program may use at most 128 MiB of HBM per device.

v0:
```python
import math
import jax
import jax.numpy as jnp
from jax import lax
from jax.sharding import PartitionSpec as P

NX = 2048
NY = 2048
depth_step = 10.0
grid_step = 25.0
freq_step = 0.0625
highest = lax.Precision.HIGHEST
first_factor = 32


def extended(cells, sides, width):
    for axis, dim in sides:
        count = lax.axis_size(axis)
        ends = count - 1
        head = lax.slice_in_dim(cells, 0, width, axis=dim)
        tail = lax.slice_in_dim(cells, cells.shape[dim] - width, cells.shape[dim], axis=dim)
        cells = jnp.concatenate(
            [
                lax.ppermute(tail, axis, [(i, (i + 1) % count) for i in range(ends)]),
                cells,
                lax.ppermute(head, axis, [((i + 1) % count, i) for i in range(ends)]),
            ],
            axis=dim,
        )
    return cells


def fourier_tables(count):
    indices = lax.iota(jnp.int32, count)
    product = indices[:, None] * indices[None, :] % count
    angles = 2.0 * math.pi / count * product.astype(jnp.float32)
    return (jnp.cos(angles), jnp.sin(angles))


def twiddle_tables(outer, inner, count):
    left = lax.iota(jnp.int32, outer)
    right = lax.iota(jnp.int32, inner)
    product = left[:, None] * right[None, :] % count
    angles = 2.0 * math.pi / count * product.astype(jnp.float32)
    return (jnp.cos(angles), jnp.sin(angles))


def signed_waves(indices, count):
    signed = jnp.where(indices < count // 2, indices, indices - count)
    return 2.0 * math.pi / (count * grid_step) * signed.astype(jnp.float32)


def table_product(form, cos_t, sin_t, real, imag, sign):
    new_real = jnp.einsum(form, cos_t, real, precision=highest) - sign * jnp.einsum(
        form, sin_t, imag, precision=highest
    )
    new_imag = jnp.einsum(form, cos_t, imag, precision=highest) + sign * jnp.einsum(
        form, sin_t, real, precision=highest
    )
    return (new_real, new_imag)


def transform_axis(real, imag, sign, middle):
    if middle:
        members, count, other = real.shape
    else:
        members, other, count = real.shape
    inner = count // first_factor
    cos_a, sin_a = fourier_tables(first_factor)
    cos_b, sin_b = fourier_tables(inner)
    tw_cos, tw_sin = twiddle_tables(first_factor, inner, count)
    if middle:
        real = real.reshape(members, first_factor, inner, other)
        imag = imag.reshape(members, first_factor, inner, other)
        real, imag = table_product("ka,fabc->fkbc", cos_a, sin_a, real, imag, sign)
        tw_cos = tw_cos[None, :, :, None]
        tw_sin = tw_sin[None, :, :, None]
        form_two = "lb,fkbc->flkc"
    else:
        real = real.reshape(members, other, first_factor, inner)
        imag = imag.reshape(members, other, first_factor, inner)
        real, imag = table_product("ka,frab->frkb", cos_a, sin_a, real, imag, sign)
        tw_cos = tw_cos[None, None]
        tw_sin = tw_sin[None, None]
        form_two = "lb,frkb->frlk"
    turned_real = real * tw_cos - sign * imag * tw_sin
    turned_imag = imag * tw_cos + sign * real * tw_sin
    real, imag = table_product(form_two, cos_b, sin_b, turned_real, turned_imag, sign)
    if middle:
        return (real.reshape(members, count, other), imag.reshape(members, count, other))
    return (real.reshape(members, other, count), imag.reshape(members, other, count))


def spectral_step(real_part, imag_part, angular, mean_slow):
    total_y = real_part.shape[2]
    fwd_real, fwd_imag = transform_axis(real_part, imag_part, -1.0, False)
    columns = lax.all_to_all(
        jnp.stack([fwd_real, fwd_imag]), "lat", split_axis=3, concat_axis=2, tiled=True
    )
    total_x = columns.shape[2]
    spec_real, spec_imag = transform_axis(columns[0], columns[1], -1.0, True)
    width = columns.shape[3]
    col_index = lax.axis_index("lat") * width + lax.iota(jnp.int32, width)
    wave_y = signed_waves(col_index, total_y)
    wave_x = signed_waves(lax.iota(jnp.int32, total_x), total_x)
    vertical = (
        (angular * mean_slow)[:, None, None] ** 2
        - wave_x[None, :, None] ** 2
        - wave_y[None, None, :] ** 2
    )
    damping = jnp.exp(-jnp.sqrt(jnp.maximum(-vertical, 0.0)) * depth_step)
    advance = jnp.sqrt(jnp.maximum(vertical, 0.0)) * depth_step
    turn_real = damping * jnp.cos(advance)
    turn_imag = damping * jnp.sin(advance)
    shift_real = spec_real * turn_real - spec_imag * turn_imag
    shift_imag = spec_real * turn_imag + spec_imag * turn_real
    back_real, back_imag = transform_axis(shift_real, shift_imag, 1.0, True)
    back_real = back_real / total_x
    back_imag = back_imag / total_x
    strips = lax.all_to_all(
        jnp.stack([back_real, back_imag]), "lat", split_axis=2, concat_axis=3, tiled=True
    )
    out_real, out_imag = transform_axis(strips[0], strips[1], 1.0, False)
    return (out_real / total_y, out_imag / total_y)


def local(wavefield, source_field, slowness, freq_index):
    members = wavefield.shape[1]
    strip = lax.all_gather(slowness, "freq", axis=1, tiled=True)
    total = lax.psum(jnp.sum(strip), "lat")
    mean_slow = total / (NX * NY)
    angular = 2.0 * math.pi * freq_step * freq_index.astype(jnp.float32)
    lens_angle = angular[:, None, None] * (strip - mean_slow)[None] * depth_step
    lens_cos = jnp.cos(lens_angle)
    lens_sin = jnp.sin(lens_angle)
    real_part = wavefield[0] * lens_cos - wavefield[1] * lens_sin
    imag_part = wavefield[0] * lens_sin + wavefield[1] * lens_cos
    prop_real, prop_imag = spectral_step(real_part, imag_part, angular, mean_slow)
    stacked = jnp.stack([prop_real, prop_imag])
    padded = extended(stacked, (("lat", 2),), 1)
    side_pad = jnp.pad(stacked, ((0, 0), (0, 0), (0, 0), (1, 1)))
    beside_all = (
        padded[:, :, 2:, :] + padded[:, :, :-2, :] + side_pad[:, :, :, 2:] + side_pad[:, :, :, :-2]
    )
    laplace = beside_all - 4.0 * stacked
    lateral_gain = (
        depth_step
        * (
            0.5 / (angular[:, None, None] * mean_slow)
            - 0.5 / (angular[:, None, None] * strip[None])
        )
        / (grid_step * grid_step)
    )
    new_real = prop_real + lateral_gain * laplace[1]
    new_imag = prop_imag - lateral_gain * laplace[0]
    batch_total = members * lax.axis_size("freq")
    terms = jnp.sum(new_real * source_field[0] + new_imag * source_field[1], axis=0) / math.sqrt(
        batch_total
    )
    image = lax.psum_scatter(terms, "freq", scatter_dimension=1, tiled=True)
    return (jnp.stack([new_real, new_imag]), image)


def solution(mesh):
    return jax.shard_map(
        local,
        mesh=mesh,
        in_specs=(
            P(None, "freq", "lat", None),
            P(None, "freq", "lat", None),
            P("lat", "freq"),
            P("freq"),
        ),
        out_specs=(P(None, "freq", "lat", None), P("lat", "freq")),
        check_vma=False,
    )
```

profile of v0, /device:TPU:0, one launch (start us, length us, event | category | flops | bytes accessed | tf_op | source)
XLA Modules:
  0.0 928.1 jit_solution(8928447778791640208)
XLA Ops:
  9.3 8.0 fusion.360
  22.8 25.7 %all-gather.2.cloned.1.call-done = f32[256,2048]{0,1:T(8,128)} async-done(((f32[256,512]{0,1:T(8,128)}), f32[256,2048]{0,1:T(8,128)}) %all-gather.2.cloned.1.call-update) | async-done | bytes 2097168 | tf_op jit(solution)/shard_map/all_gather | solution.py:129
  56.7 17.0 %psum.7 = f32[]{:T(128)} all-reduce(f32[]{:T(128)} %reduce_sum.18), channel_id=1, replica_groups=mesh['lat'=8,'freq'=4] {'lat'}, use_global_device_ids=true, to_apply=%region_1.0 | all-reduce | flops 1 | bytes 8 | tf_op jit(solution)/shard_map/psum | solution.py:130
  77.2 17.5 %multiply_subtract_fusion.3 = (f32[2,256,32,64]{1,3,2,0:T(8,128)S(1)}, f32[2,256,32,64]{1,3,2,0:T(8,128)S(1)}) fusion(f32[2,256,32,64]{1,3,2,0:T(8,128)} %bitcast.236, f32[2,256,32,64]{1,3,2,0:T(8,128)S(1)} %bitcast.235, f32[256,32,64]{0,2,1:T(8,128)S(1)} %bitcast.243, f32[2]{0:T(128)S(1)} %get-tuple-element.34), kind=kLoop, calls=%fused_computation.85 | loop fusion | flops 8388608 | bytes 18874376 | tf_op jit(solution)/shard_map/sub | solution.py:136
  101.3 7.2 fusion.89
  115.4 8.3 fusion.29
  130.3 7.0 fusion.81
  156.9 16.5 %copy.145 = f32[2,2,256,2048]{2,1,0,3:T(2,128)} copy(f32[2,2,256,2048]{2,3,1,0:T(8,128)S(1)} %pad_maximum_fusion.5) | data formatting | bytes 16777216 | tf_op jit(solution)/shard_map/stack | solution.py:98
  179.0 183.6 %all-to-all-done = f32[2,2,256,2048]{2,1,0,3:T(2,128)} async-done(((f32[2,2,256,2048]{2,1,0,3:T(2,128)}), f32[2,2,256,2048]{2,1,0,3:T(2,128)}, u32[]{:S(2)}, u32[]{:S(2)}) %all-to-all-start) | async-done | bytes 8388640 | tf_op jit(solution)/shard_map/all_to_all | solution.py:97
  377.0 10.4 %fusion.75 = f32[2,64,256,32]{2,3,1,0:T(8,128)} fusion(f32[2,32,64,256]{3,2,1,0:T(8,128)} %bitcast.229), kind=kOutput, calls=%fused_computation.131 | convolution fusion | flops 402667520 | bytes 8388608 | tf_op jit(solution)/shard_map/ka,fabc->fkbc/dot_general | solution.py:54
  387.4 7.1 fusion.73
  400.1 10.3 %multiply_subtract_fusion.1 = f32[2,64,256,32]{2,3,1,0:T(8,128)S(1)} fusion(f32[2,64,256,32]{2,3,1,0:T(8,128)} %fusion.75, f32[2,32,64,256]{3,2,1,0:T(8,128)} %bitcast.227), kind=kOutput, calls=%fused_computation.79 | convolution fusion | flops 404764672 | bytes 12582912 | tf_op jit(solution)/shard_map/ka,fabc->fkbc/dot_general | solution.py:54
  410.4 8.4 fusion.27
  425.3 7.1 fusion.65
  441.8 7.2 add_bitcast_fusion
  451.4 19.5 %fusion.25 = (f32[2,32,64,256]{3,2,1,0:T(8,128)S(1)}, f32[2,32,64,256]{3,2,1,0:T(8,128)S(1)}) fusion(f32[256]{0:T(256)S(1)} %fusion.226, f32[2,32,64]{2,1,0:T(8,128)S(1)} %broadcast_subtract_fusion.1, f32[2,32,64,256]{3,2,1,0:T(8,128)S(1)} %bitcast.239, f32[2,32,64,256]{3,2,1,0:T(8,128)S(1)} %bitcast.237), kind=kLoop, calls=%fused_computation.53 | loop fusion | flops 15728640 | bytes 16794624 | tf_op jit(solution)/shard_map/sub | solution.py:115
  477.6 7.1 fusion.57
  491.4 8.4 fusion.23
  532.9 16.7 %copy.169 = f32[2,2,2048,256]{3,1,0,2:T(2,128)} copy(f32[2,2,2048,256]{3,2,1,0:T(8,128)S(1)} %pad_maximum_fusion.6) | data formatting | bytes 16777216 | tf_op jit(solution)/shard_map/stack | solution.py:121
  554.6 7.8 fusion.357
  573.2 165.3 %all-to-all-done.1 = f32[2,2,2048,256]{3,1,0,2:T(2,128)} async-done(((f32[2,2,2048,256]{3,1,0,2:T(2,128)}), f32[2,2,2048,256]{3,1,0,2:T(2,128)}, u32[]{:S(2)}, u32[]{:S(2)}) %all-to-all-start.1) | async-done | bytes 8388640 | tf_op jit(solution)/shard_map/all_to_all | solution.py:120
  752.8 10.4 %fusion.43 = f32[2,256,64,32]{1,3,2,0:T(8,128)} fusion(f32[2,256,32,64]{1,3,2,0:T(8,128)} %bitcast.231), kind=kOutput, calls=%fused_computation.99 | convolution fusion | flops 402667520 | bytes 8388608 | tf_op jit(solution)/shard_map/ka,frab->frkb/dot_general | solution.py:54
  763.3 7.5 fusion.41
  776.1 10.4 %fusion.103 = f32[2,256,64,32]{1,3,2,0:T(8,128)S(1)} fusion(f32[2,256,64,32]{1,3,2,0:T(8,128)} %fusion.43, f32[2,256,32,64]{1,3,2,0:T(8,128)} %bitcast.225), kind=kOutput, calls=%fused_computation.155 | convolution fusion | flops 403716096 | bytes 12582912 | tf_op jit(solution)/shard_map/ka,frab->frkb/dot_general | solution.py:54
  786.5 8.4 fusion.21
  808.3 7.0 multiply_bitcast_fusion
  817.8 7.3 multiply_bitcast_fusion.1
  842.2 7.4 pad_maximum_fusion
  855.1 21.9 %fusion.3 = f32[2,2,256,2048]{2,3,1,0:T(8,128)} fusion(f32[2,2,1,2048]{2,3,1,0:T(8,128)} %copy.186, f32[1,2,256,2048]{2,3,1,0:T(8,128)} %bitcast.221, f32[1,2,256,2048]{2,3,1,0:T(8,128)} %bitcast.224, f32[2,2,1,2048]{2,3,1,0:T(8,128)} %copy.184, f32[2,2,256,2048]{2,3,1,0:T(8,128)} %pad_maximum_fusion), kind=kLoop, calls=%fused_computation.9 | loop fusion | flops 18874368 | bytes 25231360 | tf_op jit(solution)/shard_map/sub | solution.py:145
  877.0 7.2 fusion.18
  896.7 8.7 copy.191
  905.4 13.6 %reduce-scatter.2.cloned.1.call-done = f32[256,512]{0,1:T(8,128)} async-done(((f32[256,2048]{0,1:T(8,128)}), f32[256,512]{0,1:T(8,128)}) %reduce-scatter.2.cloned.1.call-update) | async-done | bytes 524304 | tf_op jit(solution)/shard_map/reduce_scatter | solution.py:160
  (99 shorter events, 236.2 us)
Async XLA Ops:
  7.2 41.3 %all-gather.2.cloned.1.call-start = ((), (), s32[]{:S(2)}) async-start(), calls=%async_computation.3 | async-start | bytes 2621440 | tf_op jit(solution)/shard_map/all_gather | solution.py:129
  51.2 23.8 %copy-start.16 = (s32[2]{0:T(128)S(1)}, s32[2]{0:T(128)}, u32[]{:S(2)}) copy-start(s32[2]{0:T(128)} %param.7) | copy-start | bytes 28
  51.2 24.3 %copy-start.8 = (f32[256,2048]{0,1:T(8,128)S(1)}, f32[256,2048]{0,1:T(8,128)}, u32[]{:S(2)}) copy-start(f32[256,2048]{0,1:T(8,128)} %all-gather.2.cloned.1.call-done) | copy-start | bytes 6291460
  75.0 2.2 copy-start.12
  75.5 19.2 %copy-start.13 = (f32[2]{0:T(128)}, f32[2]{0:T(128)S(1)}, u32[]{:S(2)}) copy-start(f32[2]{0:T(128)S(1)} %get-tuple-element.34) | copy-start | bytes 28
  173.4 189.3 %all-to-all-start = ((f32[2,2,256,2048]{2,1,0,3:T(2,128)}), f32[2,2,256,2048]{2,1,0,3:T(2,128)}, u32[]{:S(2)}, u32[]{:S(2)}) async-start(f32[2,2,256,2048]{2,1,0,3:T(2,128)} %copy.145), calls=%async_computation | async-start | bytes 16777216 | tf_op jit(solution)/shard_map/all_to_all | solution.py:97
  377.0 10.4 %copy-start.6 = (f32[1,2,8,256,256]{4,3,2,1,0:T(8,128)S(1)}, f32[1,2,8,256,256]{4,3,2,1,0:T(8,128)}, u32[]{:S(2)}) copy-start(f32[1,2,8,256,256]{4,3,2,1,0:T(8,128)} %copy.149) | copy-start | bytes 12582916
  400.0 10.4 %copy-start.5 = (f32[1,2,8,256,256]{4,3,2,1,0:T(8,128)S(1)}, f32[1,2,8,256,256]{4,3,2,1,0:T(8,128)}, u32[]{:S(2)}) copy-start(f32[1,2,8,256,256]{4,3,2,1,0:T(8,128)} %copy.147) | copy-start | bytes 12582916
  400.0 10.4 %copy-start.11 = (f32[2,64,256,32]{2,3,1,0:T(8,128)S(1)}, f32[2,64,256,32]{2,3,1,0:T(8,128)}, u32[]{:S(2)}) copy-start(f32[2,64,256,32]{2,3,1,0:T(8,128)} %fusion.73) | copy-start | bytes 12582916
  549.6 188.9 %all-to-all-start.1 = ((f32[2,2,2048,256]{3,1,0,2:T(2,128)}), f32[2,2,2048,256]{3,1,0,2:T(2,128)}, u32[]{:S(2)}, u32[]{:S(2)}) async-start(f32[2,2,2048,256]{3,1,0,2:T(2,128)} %copy.169), calls=%async_computation.1 | async-start | bytes 16777216 | tf_op jit(solution)/shard_map/all_to_all | solution.py:120
  554.6 364.5 %reduce-scatter.2.cloned.1.call-start = ((), (), s32[]{:S(2)}) async-start(), calls=%async_computation.4 | async-start | bytes 2621440 | tf_op jit(solution)/shard_map/reduce_scatter | solution.py:160
  752.8 10.5 %copy-start.7 = (f32[1,2,256,8,256]{2,4,3,1,0:T(8,128)S(1)}, f32[1,2,256,8,256]{2,4,3,1,0:T(8,128)}, u32[]{:S(2)}) copy-start(f32[1,2,256,8,256]{2,4,3,1,0:T(8,128)} %copy.173) | copy-start | bytes 12582916
  776.1 10.4 %copy-start.4 = (f32[1,2,256,8,256]{2,4,3,1,0:T(8,128)S(1)}, f32[1,2,256,8,256]{2,4,3,1,0:T(8,128)}, u32[]{:S(2)}) copy-start(f32[1,2,256,8,256]{2,4,3,1,0:T(8,128)} %copy.171) | copy-start | bytes 12582916
  776.1 10.4 %copy-start.10 = (f32[2,256,64,32]{1,3,2,0:T(8,128)S(1)}, f32[2,256,64,32]{1,3,2,0:T(8,128)}, u32[]{:S(2)}) copy-start(f32[2,256,64,32]{1,3,2,0:T(8,128)} %fusion.41) | copy-start | bytes 12582916
  817.8 9.8 %copy-start = (f32[2,256,64,32]{1,3,2,0:T(8,128)}, f32[2,256,64,32]{1,3,2,0:T(8,128)S(1)}, u32[]{:S(2)}) copy-start(f32[2,256,64,32]{1,3,2,0:T(8,128)S(1)} %copy.182) | copy-start | bytes 12582916
  827.6 4.6 copy-start.2
  835.0 14.6 %collective-permute-start = (f32[2,2,1,2048]{3,1,2,0:T(2,128)S(1)}, f32[2,2,1,2048]{3,1,2,0:T(2,128)S(1)}, u32[]{:S(2)}, u32[]{:S(2)}) collective-permute-start(f32[2,2,1,2048]{3,1,2,0:T(2,128)S(1)} %copy.183), channel_id=1, source_target_pairs={{4,0},{8,4},{12,8},{16,12},{20,16},{24,20},{28,24},{5,1},{9,5},{13... | collective-permute-start | bytes 98312 | tf_op jit(solution)/shard_map/ppermute | solution.py:26
  839.2 13.2 %collective-permute-start.1 = (f32[2,2,1,2048]{3,1,2,0:T(2,128)S(1)}, f32[2,2,1,2048]{3,1,2,0:T(2,128)S(1)}, u32[]{:S(2)}, u32[]{:S(2)}) collective-permute-start(f32[2,2,1,2048]{3,1,2,0:T(2,128)S(1)} %copy.185), channel_id=1, source_target_pairs={{0,4},{4,8},{8,12},{12,16},{16,20},{20,24},{24,28},{1,5},{5,9},{9,... | collective-permute-start | bytes 98312 | tf_op jit(solution)/shard_map/ppermute | solution.py:24
  855.0 21.9 %copy-start.1 = (f32[2,256,64,32]{1,3,2,0:T(8,128)S(1)}, f32[2,256,64,32]{1,3,2,0:T(8,128)}, u32[]{:S(2)}) copy-start(f32[2,256,64,32]{1,3,2,0:T(8,128)} %copy-done) | copy-start | bytes 12582916
  855.1 21.9 %copy-start.3 = (f32[2,256,64,32]{1,3,2,0:T(8,128)S(1)}, f32[2,256,64,32]{1,3,2,0:T(8,128)}, u32[]{:S(2)}) copy-start(f32[2,256,64,32]{1,3,2,0:T(8,128)} %copy-done.2) | copy-start | bytes 12582916
  855.1 21.9 %copy-start.9 = (f32[256,2048]{0,1:T(8,128)S(1)}, f32[256,2048]{0,1:T(8,128)}, u32[]{:S(2)}) copy-start(f32[256,2048]{0,1:T(8,128)} %all-gather.2.cloned.1.call-done) | copy-start | bytes 6291460
  855.1 21.9 %copy-start.14 = (f32[2]{0:T(128)S(1)}, f32[2]{0:T(128)}, u32[]{:S(2)}) copy-start(f32[2]{0:T(128)} %copy-done.13) | copy-start | bytes 28
  855.1 21.9 %copy-start.15 = (f32[2]{0:T(128)S(1)}, f32[2]{0:T(128)}, u32[]{:S(2)}) copy-start(f32[2]{0:T(128)} %get-tuple-element.32) | copy-start | bytes 28
Sparse Core Ops, SparseCore 0:
  10.4 38.0 all-gather.1
  885.9 33.0 reduce-scatter.1
where the time goes:
time: 933 us; the launch traced here: 928 us
  waiting for transfers between devices  388 us (42%)
  matrix products  241 us (26%)
  local copies, waits for them, and re-layouts  156 us (17%)
  other arithmetic  95.3 us (10%)
  blocking collectives  17 us (2%)
  between operations  16.1 us (2%)
  starting transfers between devices  14.7 us (2%)
    all_to_all x1, waiting for transfers between devices, spectral_step(): lax.all_to_all(jnp.stack([fwd_real, fwd_imag]), 'lat', split_axis=3, conc...  184 us
    all_to_all x1, waiting for transfers between devices, spectral_step(): lax.all_to_all(jnp.stack([back_real, back_imag]), 'lat', split_axis=2, co...  165 us
    dot_general x8, matrix products, table_product(): jnp.einsum(form, cos_t, real, precision=highest)  62.6 us
    dot_general x8, matrix products, table_product(): jnp.einsum(form, sin_t, real, precision=highest)  61.6 us
    dot_general x8, matrix products, table_product(): jnp.einsum(form, sin_t, imag, precision=highest)  60.6 us
    dot_general x8, matrix products, table_product(): jnp.einsum(form, cos_t, imag, precision=highest)  56.2 us
    unnamed x41, local copies, waits for them, and re-layouts  36.1 us
    all_gather x1, waiting for transfers between devices, local(): strip = lax.all_gather(slowness, 'freq', axis=1, tiled=True)  25.7 us
  transfers between devices with their start and end apart: 6, of which 4 were waited for; matrix products, arithmetic and copies ran while one was open for 7% of the time, Pallas kernels for 0%

commit v1 on v0

--- a/solution.py
+++ b/solution.py
@@ -1,3 +1,4 @@
+import functools
 import math
 import jax
 import jax.numpy as jnp
@@ -11,6 +12,34 @@
 freq_step = 0.0625
 highest = lax.Precision.HIGHEST
 first_factor = 32
+
+
+def _compute_samples(x_local, dim_k, x_in):
+    z = x_local.shape
+    tall = x_local.reshape(*z[:dim_k], x_in, z[dim_k] // x_in, *z[dim_k + 1 :])
+    return jnp.moveaxis(tall, dim_k, 0)
+
+
+def do_the_arrays(my_data, dim_no):
+    top = list(my_data.shape[1:])
+    top[dim_no] *= my_data.shape[0]
+    return jnp.moveaxis(my_data, 0, dim_no).reshape(top)
+
+
+def pair_hubs(block_here, ax_name, patch, array_here):
+    now, frame_out = (lax.axis_size(ax_name), lax.axis_index(ax_name))
+    local_now = _compute_samples(block_here, patch, now)
+    ledger = [local_now[frame_out]]
+    for kk in tuple(range(1, now)):
+        then = local_now[frame_out ^ kk]
+        arr_next = lax.ppermute(then, ax_name, [(k0, k0 ^ kk) for k0 in range(now)])
+        ledger.append(arr_next)
+    block_out = jnp.stack(ledger, axis=0)
+    local_now = block_out[frame_out ^ jnp.arange(now)]
+    return do_the_arrays(local_now, array_here)
+
+
+sizes_part = functools.partial(pair_hubs, ax_name="lat", patch=3, array_here=2)
 
 
 def extended(cells, sides, width):
@@ -94,9 +123,7 @@
 def spectral_step(real_part, imag_part, angular, mean_slow):
     total_y = real_part.shape[2]
     fwd_real, fwd_imag = transform_axis(real_part, imag_part, -1.0, False)
-    columns = lax.all_to_all(
-        jnp.stack([fwd_real, fwd_imag]), "lat", split_axis=3, concat_axis=2, tiled=True
-    )
+    columns = sizes_part(jnp.stack([fwd_real, fwd_imag]))
     total_x = columns.shape[2]
     spec_real, spec_imag = transform_axis(columns[0], columns[1], -1.0, True)
     width = columns.shape[3]

time: 933 us -> 902 us (0.967)
  waiting for transfers between devices: 388 us -> 318 us
  starting transfers between devices: 14.7 us -> 49.8 us
    all_to_all x1 -> x0, waiting for transfers between devices: 184 us -> none  [spectral_step(): lax.all_to_all(jnp.stack([fwd_real, fwd_imag]), 'lat', split_axis=3, conc...]
    ppermute x0 -> x7, waiting for transfers between devices: none -> 118 us  [pair_hubs(): arr_next = lax.ppermute(then, ax_name, [(k0, k0 ^ kk) for k0 in range(now)])]
    all_to_all x1, starting transfers between devices: 4.96 us -> 40.1 us  [spectral_step(): lax.all_to_all(jnp.stack([back_real, back_imag]), 'lat', split_axis=2, co...]
    unnamed x41 -> x44, local copies, waits for them, and re-layouts: 36.1 us -> 48.9 us
    slice x3, local copies, waits for them, and re-layouts: 14.9 us -> 5.18 us  [spectral_step(): spec_real, spec_imag = transform_axis(columns[0], columns[1], -1.0, True)]
  transfers between devices with their start and end apart: 6 -> 12, of which waited for: 4 -> 6; matrix products, arithmetic and copies ran while one was open for 7% -> 11% of each run, Pallas kernels for 0% -> 0%
where the time goes in v1:
time: 902 us; the launch traced here: 897 us
  waiting for transfers between devices  318 us (35%)
  matrix products  234 us (26%)
  local copies, waits for them, and re-layouts  160 us (18%)
  other arithmetic  101 us (11%)
  starting transfers between devices  49.8 us (6%)
  blocking collectives  17 us (2%)
  between operations  16.1 us (2%)
    all_to_all x1, waiting for transfers between devices, spectral_step(): lax.all_to_all(jnp.stack([back_real, back_imag]), 'lat', split_axis=2, co...  166 us
    ppermute x7, waiting for transfers between devices, pair_hubs(): arr_next = lax.ppermute(then, ax_name, [(k0, k0 ^ kk) for k0 in range(now)])  118 us
    dot_general x8, matrix products, table_product(): jnp.einsum(form, sin_t, real, precision=highest)  61.9 us
    dot_general x8, matrix products, table_product(): jnp.einsum(form, cos_t, real, precision=highest)  59.6 us
    dot_general x8, matrix products, table_product(): jnp.einsum(form, sin_t, imag, precision=highest)  57.2 us
    dot_general x8, matrix products, table_product(): jnp.einsum(form, cos_t, imag, precision=highest)  55.2 us
    unnamed x44, local copies, waits for them, and re-layouts  48.9 us
    all_to_all x1, starting transfers between devices, spectral_step(): lax.all_to_all(jnp.stack([back_real, back_imag]), 'lat', split_axis=2, co...  40.1 us
  transfers between devices with their start and end apart: 12, of which 6 were waited for; matrix products, arithmetic and copies ran while one was open for 11% of the time, Pallas kernels for 0%

profile of v1, /device:TPU:0, one launch (start us, length us, event | category | flops | bytes accessed | tf_op | source)
XLA Modules:
  0.0 896.6 jit_solution(8383530016802950509)
XLA Ops:
  9.3 8.0 fusion.369
  28.3 20.2 %all-gather.2.cloned.1.call-done = f32[256,2048]{0,1:T(8,128)} async-done(((f32[256,512]{0,1:T(8,128)}), f32[256,2048]{0,1:T(8,128)}) %all-gather.2.cloned.1.call-update) | async-done | bytes 2097168 | tf_op jit(solution)/shard_map/all_gather | solution.py:156
  51.2 17.0 %psum.7 = f32[]{:T(128)} all-reduce(f32[]{:T(128)} %reduce_sum.18), channel_id=1, replica_groups=mesh['lat'=8,'freq'=4] {'lat'}, use_global_device_ids=true, to_apply=%region_1.0 | all-reduce | flops 1 | bytes 8 | tf_op jit(solution)/shard_map/psum | solution.py:157
  72.3 17.5 %multiply_subtract_fusion.3 = (f32[2,256,32,64]{1,3,2,0:T(8,128)S(1)}, f32[2,256,32,64]{1,3,2,0:T(8,128)S(1)}) fusion(f32[2,256,32,64]{1,3,2,0:T(8,128)} %bitcast.263, f32[2,256,32,64]{1,3,2,0:T(8,128)S(1)} %bitcast.262, f32[256,32,64]{0,2,1:T(8,128)S(1)} %bitcast.268, f32[2]{0:T(128)S(1)} %get-tuple-element.44), kind=kLoop, calls=%fused_computation.101 | loop fusion | flops 8388608 | bytes 18874376 | tf_op jit(solution)/shard_map/sub | solution.py:163
  96.5 7.2 fusion.89
  110.5 8.3 fusion.29
  132.3 7.2 add_bitcast_fusion.1
  179.4 21.0 %collective-permute-done.1 = f32[2,2,256,256]{3,2,1,0:T(8,128)} collective-permute-done((f32[2,2,256,256]{3,2,1,0:T(8,128)}, f32[2,2,256,256]{3,2,1,0:T(8,128)}, u32[]{:S(2)}, u32[]{:S(2)}) %collective-permute-start.1) | collective-permute-done | bytes 1048608 | tf_op jit(solution)/shard_map/ppermute | solution.py:35
  203.3 41.2 %collective-permute-done.2 = f32[2,2,256,256]{3,2,1,0:T(8,128)} collective-permute-done((f32[2,2,256,256]{3,2,1,0:T(8,128)}, f32[2,2,256,256]{3,2,1,0:T(8,128)}, u32[]{:S(2)}, u32[]{:S(2)}) %collective-permute-start.2) | collective-permute-done | bytes 1048608 | tf_op jit(solution)/shard_map/ppermute | solution.py:35
  246.8 55.8 %collective-permute-done.3 = f32[2,2,256,256]{3,2,1,0:T(8,128)} collective-permute-done((f32[2,2,256,256]{3,2,1,0:T(8,128)}, f32[2,2,256,256]{3,2,1,0:T(8,128)}, u32[]{:S(2)}, u32[]{:S(2)}) %collective-permute-start.3) | collective-permute-done | bytes 1048608 | tf_op jit(solution)/shard_map/ppermute | solution.py:35
  309.2 7.7 gather_fusion
  342.6 8.5 fusion.27
  364.5 7.4 subtract_bitcast_fusion
  384.0 19.3 %fusion.25 = (f32[2,32,64,256]{3,2,1,0:T(8,128)S(1)}, f32[2,32,64,256]{3,2,1,0:T(8,128)S(1)}) fusion(f32[256]{0:T(256)S(1)} %fusion.266, f32[2,32,64]{2,1,0:T(8,128)S(1)} %broadcast_subtract_fusion.1, f32[2,32,64,256]{3,2,1,0:T(8,128)S(1)} %bitcast.265, f32[2,32,64,256]{3,2,1,0:T(8,128)S(1)} %bitcast.264), kind=kLoop, calls=%fused_computation.69 | loop fusion | flops 15728640 | bytes 16794624 | tf_op jit(solution)/shard_map/sub | solution.py:142
  410.0 7.1 fusion.57
  423.7 8.4 fusion.23
  455.3 7.0 multiply_bitcast_fusion.2
  465.3 16.7 %copy.242 = f32[2,2,2048,256]{3,1,0,2:T(2,128)} copy(f32[2,2,2048,256]{3,2,1,0:T(8,128)S(1)} %pad_maximum_fusion.5) | data formatting | bytes 16777216 | tf_op jit(solution)/shard_map/stack | solution.py:148
  482.0 40.1 %all-to-all-start = ((f32[2,2,2048,256]{3,1,0,2:T(2,128)}), f32[2,2,2048,256]{3,1,0,2:T(2,128)}, u32[]{:S(2)}, u32[]{:S(2)}) async-start(f32[2,2,2048,256]{3,1,0,2:T(2,128)} %copy.242), calls=%async_computation | async-start | bytes 16777216 | tf_op jit(solution)/shard_map/all_to_all | solution.py:147
  522.1 7.8 fusion.366
  540.7 166.2 %all-to-all-done = f32[2,2,2048,256]{3,1,0,2:T(2,128)} async-done(((f32[2,2,2048,256]{3,1,0,2:T(2,128)}), f32[2,2,2048,256]{3,1,0,2:T(2,128)}, u32[]{:S(2)}, u32[]{:S(2)}) %all-to-all-start) | async-done | bytes 8388640 | tf_op jit(solution)/shard_map/all_to_all | solution.py:147
  721.2 10.4 %fusion.43 = f32[2,256,64,32]{1,3,2,0:T(8,128)} fusion(f32[2,256,32,64]{1,3,2,0:T(8,128)} %bitcast.254), kind=kOutput, calls=%fused_computation.115 | convolution fusion | flops 402667520 | bytes 8388608 | tf_op jit(solution)/shard_map/ka,frab->frkb/dot_general | solution.py:83
  731.6 7.4 fusion.41
  744.4 10.4 %fusion.103 = f32[2,256,64,32]{1,3,2,0:T(8,128)S(1)} fusion(f32[2,256,64,32]{1,3,2,0:T(8,128)} %fusion.43, f32[2,256,32,64]{1,3,2,0:T(8,128)} %bitcast.248), kind=kOutput, calls=%fused_computation.171 | convolution fusion | flops 403716096 | bytes 12582912 | tf_op jit(solution)/shard_map/ka,frab->frkb/dot_general | solution.py:83
  754.9 8.4 fusion.21
  776.7 7.0 multiply_bitcast_fusion
  786.2 7.3 multiply_bitcast_fusion.1
  810.6 7.4 pad_maximum_fusion
  823.5 21.9 %fusion.3 = f32[2,2,256,2048]{2,3,1,0:T(8,128)} fusion(f32[2,2,1,2048]{2,3,1,0:T(8,128)} %copy.259, f32[1,2,256,2048]{2,3,1,0:T(8,128)} %bitcast.244, f32[1,2,256,2048]{2,3,1,0:T(8,128)} %bitcast.247, f32[2,2,1,2048]{2,3,1,0:T(8,128)} %copy.257, f32[2,2,256,2048]{2,3,1,0:T(8,128)} %pad_maximum_fusion), kind=kLoop, calls=%fused_computation.26 | loop fusion | flops 18874368 | bytes 25231360 | tf_op jit(solution)/shard_map/sub | solution.py:172
  845.4 7.2 fusion.18
  865.1 8.7 copy.264
  873.8 13.7 %reduce-scatter.2.cloned.1.call-done = f32[256,512]{0,1:T(8,128)} async-done(((f32[256,2048]{0,1:T(8,128)}), f32[256,512]{0,1:T(8,128)}) %reduce-scatter.2.cloned.1.call-update) | async-done | bytes 524304 | tf_op jit(solution)/shard_map/reduce_scatter | solution.py:187
  (125 shorter events, 271.0 us)
Async XLA Ops:
  7.2 41.3 %all-gather.2.cloned.1.call-start = ((), (), s32[]{:S(2)}) async-start(), calls=%async_computation.2 | async-start | bytes 2621440 | tf_op jit(solution)/shard_map/all_gather | solution.py:156
  22.7 46.7 %copy-start.14 = (s32[2]{0:T(128)S(1)}, s32[2]{0:T(128)}, u32[]{:S(2)}) copy-start(s32[2]{0:T(128)} %param.7) | copy-start | bytes 28
  69.5 2.8 copy-start.10
  70.0 19.8 %copy-start.11 = (f32[2]{0:T(128)}, f32[2]{0:T(128)S(1)}, u32[]{:S(2)}) copy-start(f32[2]{0:T(128)S(1)} %get-tuple-element.44) | copy-start | bytes 28
  142.3 9.5 %copy-start.6 = (f32[2,256,64,32]{1,3,2,0:T(8,128)}, f32[2,256,64,32]{1,3,2,0:T(8,128)S(1)}, u32[]{:S(2)}) copy-start(f32[2,256,64,32]{1,3,2,0:T(8,128)S(1)} %copy.211) | copy-start | bytes 12582916
  151.8 3.0 copy-start.7
  157.3 19.8 %collective-permute-start = (f32[2,2,256,256]{3,2,1,0:T(8,128)}, f32[2,2,256,256]{3,2,1,0:T(8,128)}, u32[]{:S(2)}, u32[]{:S(2)}) collective-permute-start(f32[2,2,256,256]{3,2,1,0:T(8,128)} %bitcast.269), channel_id=1, source_target_pairs={{0,4},{4,0},{8,12},{12,8},{16,20},{20,16},{24,28},{28,24},{1,5},{5... | collective-permute-start | bytes 3145736 | tf_op jit(solution)/shard_map/ppermute | solution.py:35
  158.8 41.6 %collective-permute-start.1 = (f32[2,2,256,256]{3,2,1,0:T(8,128)}, f32[2,2,256,256]{3,2,1,0:T(8,128)}, u32[]{:S(2)}, u32[]{:S(2)}) collective-permute-start(f32[2,2,256,256]{3,2,1,0:T(8,128)} %bitcast.271), channel_id=1, source_target_pairs={{0,8},{4,12},{8,0},{12,4},{16,24},{20,28},{24,16},{28,20},{1,9},{5... | collective-permute-start | bytes 3145736 | tf_op jit(solution)/shard_map/ppermute | solution.py:35
  162.8 142.0 %collective-permute-start.4 = (f32[2,2,256,256]{3,2,1,0:T(8,128)}, f32[2,2,256,256]{3,2,1,0:T(8,128)}, u32[]{:S(2)}, u32[]{:S(2)}) collective-permute-start(f32[2,2,256,256]{3,2,1,0:T(8,128)} %bitcast.270), channel_id=1, source_target_pairs={{0,20},{4,16},{8,28},{12,24},{16,4},{20,0},{24,12},{28,8},{1,21},{... | collective-permute-start | bytes 3145736 | tf_op jit(solution)/shard_map/ppermute | solution.py:35
  167.1 77.4 %collective-permute-start.2 = (f32[2,2,256,256]{3,2,1,0:T(8,128)}, f32[2,2,256,256]{3,2,1,0:T(8,128)}, u32[]{:S(2)}, u32[]{:S(2)}) collective-permute-start(f32[2,2,256,256]{3,2,1,0:T(8,128)} %bitcast.275), channel_id=1, source_target_pairs={{0,12},{4,8},{8,4},{12,0},{16,28},{20,24},{24,20},{28,16},{1,13},{... | collective-permute-start | bytes 3145736 | tf_op jit(solution)/shard_map/ppermute | solution.py:35
  170.3 132.3 %collective-permute-start.3 = (f32[2,2,256,256]{3,2,1,0:T(8,128)}, f32[2,2,256,256]{3,2,1,0:T(8,128)}, u32[]{:S(2)}, u32[]{:S(2)}) collective-permute-start(f32[2,2,256,256]{3,2,1,0:T(8,128)} %bitcast.274), channel_id=1, source_target_pairs={{0,16},{4,20},{8,24},{12,28},{16,0},{20,4},{24,8},{28,12},{1,17},{... | collective-permute-start | bytes 3145736 | tf_op jit(solution)/shard_map/ppermute | solution.py:35
  177.1 130.1 %collective-permute-start.5 = (f32[2,2,256,256]{3,2,1,0:T(8,128)}, f32[2,2,256,256]{3,2,1,0:T(8,128)S(1)}, u32[]{:S(2)}, u32[]{:S(2)}) collective-permute-start(f32[2,2,256,256]{3,2,1,0:T(8,128)} %bitcast.273), channel_id=1, source_target_pairs={{0,24},{4,28},{8,16},{12,20},{16,8},{20,12},{24,0},{28,4},{1,25},{... | collective-permute-start | bytes 3145736 | tf_op jit(solution)/shard_map/ppermute | solution.py:35
  200.4 107.8 %collective-permute-start.6 = (f32[2,2,256,256]{3,2,1,0:T(8,128)S(1)}, f32[2,2,256,256]{3,2,1,0:T(8,128)S(1)}, u32[]{:S(2)}, u32[]{:S(2)}) collective-permute-start(f32[2,2,256,256]{3,2,1,0:T(8,128)S(1)} %bitcast.272), channel_id=1, source_target_pairs={{0,28},{4,24},{8,20},{12,16},{16,12},{20,8},{24,4},{28,0},{1,29},{... | collective-permute-start | bytes 3145736 | tf_op jit(solution)/shard_map/ppermute | solution.py:35
  482.0 224.9 %all-to-all-start = ((f32[2,2,2048,256]{3,1,0,2:T(2,128)}), f32[2,2,2048,256]{3,1,0,2:T(2,128)}, u32[]{:S(2)}, u32[]{:S(2)}) async-start(f32[2,2,2048,256]{3,1,0,2:T(2,128)} %copy.242), calls=%async_computation | async-start | bytes 16777216 | tf_op jit(solution)/shard_map/all_to_all | solution.py:147
  522.1 365.5 %reduce-scatter.2.cloned.1.call-start = ((), (), s32[]{:S(2)}) async-start(), calls=%async_computation.3 | async-start | bytes 2621440 | tf_op jit(solution)/shard_map/reduce_scatter | solution.py:187
  721.2 10.4 %copy-start.5 = (f32[1,2,256,8,256]{2,4,3,1,0:T(8,128)S(1)}, f32[1,2,256,8,256]{2,4,3,1,0:T(8,128)}, u32[]{:S(2)}) copy-start(f32[1,2,256,8,256]{2,4,3,1,0:T(8,128)} %copy.246) | copy-start | bytes 12582916
  744.4 10.4 %copy-start.4 = (f32[1,2,256,8,256]{2,4,3,1,0:T(8,128)S(1)}, f32[1,2,256,8,256]{2,4,3,1,0:T(8,128)}, u32[]{:S(2)}) copy-start(f32[1,2,256,8,256]{2,4,3,1,0:T(8,128)} %copy.244) | copy-start | bytes 12582916
  744.4 10.4 %copy-start.9 = (f32[2,256,64,32]{1,3,2,0:T(8,128)S(1)}, f32[2,256,64,32]{1,3,2,0:T(8,128)}, u32[]{:S(2)}) copy-start(f32[2,256,64,32]{1,3,2,0:T(8,128)} %fusion.41) | copy-start | bytes 12582916
  786.2 9.8 %copy-start = (f32[2,256,64,32]{1,3,2,0:T(8,128)}, f32[2,256,64,32]{1,3,2,0:T(8,128)S(1)}, u32[]{:S(2)}) copy-start(f32[2,256,64,32]{1,3,2,0:T(8,128)S(1)} %copy.255) | copy-start | bytes 12582916
  796.0 4.6 copy-start.2
  803.4 14.6 %collective-permute-start.7 = (f32[2,2,1,2048]{3,1,2,0:T(2,128)S(1)}, f32[2,2,1,2048]{3,1,2,0:T(2,128)S(1)}, u32[]{:S(2)}, u32[]{:S(2)}) collective-permute-start(f32[2,2,1,2048]{3,1,2,0:T(2,128)S(1)} %copy.256), channel_id=1, source_target_pairs={{4,0},{8,4},{12,8},{16,12},{20,16},{24,20},{28,24},{5,1},{9,5},{13... | collective-permute-start | bytes 98312 | tf_op jit(solution)/shard_map/ppermute | solution.py:55
  807.5 13.2 %collective-permute-start.8 = (f32[2,2,1,2048]{3,1,2,0:T(2,128)S(1)}, f32[2,2,1,2048]{3,1,2,0:T(2,128)S(1)}, u32[]{:S(2)}, u32[]{:S(2)}) collective-permute-start(f32[2,2,1,2048]{3,1,2,0:T(2,128)S(1)} %copy.258), channel_id=1, source_target_pairs={{0,4},{4,8},{8,12},{12,16},{16,20},{20,24},{24,28},{1,5},{5,9},{9,... | collective-permute-start | bytes 98312 | tf_op jit(solution)/shard_map/ppermute | solution.py:53
  823.4 21.9 %copy-start.1 = (f32[2,256,64,32]{1,3,2,0:T(8,128)S(1)}, f32[2,256,64,32]{1,3,2,0:T(8,128)}, u32[]{:S(2)}) copy-start(f32[2,256,64,32]{1,3,2,0:T(8,128)} %copy-done) | copy-start | bytes 12582916
  823.4 21.9 %copy-start.3 = (f32[2,256,64,32]{1,3,2,0:T(8,128)S(1)}, f32[2,256,64,32]{1,3,2,0:T(8,128)}, u32[]{:S(2)}) copy-start(f32[2,256,64,32]{1,3,2,0:T(8,128)} %copy-done.2) | copy-start | bytes 12582916
  823.4 21.9 %copy-start.8 = (f32[256,2048]{0,1:T(8,128)S(1)}, f32[256,2048]{0,1:T(8,128)}, u32[]{:S(2)}) copy-start(f32[256,2048]{0,1:T(8,128)} %all-gather.2.cloned.1.call-done) | copy-start | bytes 6291460
  823.4 21.9 %copy-start.12 = (f32[2]{0:T(128)S(1)}, f32[2]{0:T(128)}, u32[]{:S(2)}) copy-start(f32[2]{0:T(128)} %copy-done.11) | copy-start | bytes 28
  823.4 21.9 %copy-start.13 = (f32[2]{0:T(128)S(1)}, f32[2]{0:T(128)}, u32[]{:S(2)}) copy-start(f32[2]{0:T(128)} %get-tuple-element.42) | copy-start | bytes 28
Sparse Core Ops, SparseCore 0:
  10.4 38.0 all-gather.1
  854.3 33.1 reduce-scatter.1
